TPU v7x, 256 devices: a whole 4x4x8 slice. The times are simulated.
256 devices in a mesh: wide: 16 (over x, y_lo, core), deep: 16 (over z, y_hi).
Axes of the slice: x: 4, y: 4 (y_hi: 2, y_lo: 2; y = y_hi * 2 + y_lo), z: 8, core: 2. Of those that a mesh axis runs over, the one named last changes fastest.
Arguments:
- ratings: bfloat16 [131072, 4096], P(('wide', 'deep')), may hold values from -6 to 6
- recency_caps: int32 [131072, 8], P(('wide', 'deep')), may hold values from 1 to 512
- user_factors: float32 [131072, 256], P(('wide', 'deep')), may hold values from -0.75 to 0.75
- item_factors: float32 [131072, 256], P(('wide', 'deep')), may hold values from -0.75 to 0.75
- refresh_ids: int32 [32768], P(('wide', 'deep')), may hold values from 0 to 511
Outputs:
- users_out: float32 [131072, 256], P(('wide', 'deep'))
- items_out: float32 [131072, 256], P(('wide', 'deep'))
- scores: float32 [16, 2048, 8192], P('deep', None, 'wide')
Inputs may be any that keep to these rules, and one draw needn't show every extreme that they name: `recency_caps`: an item of a block counts as rated by a user in that stratum when its recency position is below the user's cap. `refresh_ids`: indices into the device's own 512 users; repeats may occur.
All inputs are finite; a program needn't handle non-finite values.
Results may differ from a plain program's by a relative error of at most 0.0003.
Values sent between devices are 32-bit elements; how exact they have to be, the bound alone decides.
A program may use at most 64 MiB of HBM per device.

v0:
```python
import functools

import jax
import jax.numpy as jnp
from jax import lax
from jax.experimental import pallas as pl
from jax.experimental.pallas import tpu as pltpu
from jax.sharding import PartitionSpec as P

STRATA = 8
USERS = 512
BLOCK = 512
RANK = 256
REFRESH = 128
N_WIDE = 16
N_DEEP = 16
X = 4
CHUNKS = 4
C = BLOCK // CHUNKS

VMEM_BYTES = 60 * 2**20

learn_rate = 0.1
penalty = 0.05

MESH = pl.DeviceIdType.MESH
F32 = jnp.float32
BF16 = jnp.bfloat16


def split(value):
    high = value.astype(BF16)
    return high, (value - high.astype(F32)).astype(BF16)


def product(left, right, dims):
    numbers = ((dims[0], dims[1]), ((), ()))
    dot = functools.partial(lax.dot_general, dimension_numbers=numbers, preferred_element_type=F32)
    return dot(left[0], right[0]) + (dot(left[0], right[1]) + dot(left[1], right[0]))


def strata_kernel(
    ratings, caps_in, users_in, items_in, ids,
    users_out, items_out, picked_out,
    rated, caps_across, caps, users, users_high, users_low, gradient, held, leaving, picked, limit, confidence,
    load_sem, rated_sem, item_send, item_recv, pick_send, pick_recv, store_sem,
):
    wide, deep = lax.axis_index("wide"), lax.axis_index("deep")
    joined = wide * N_DEEP + deep
    after = lax.rem(joined + 1, N_WIDE * N_DEEP)
    before = lax.rem(joined + N_WIDE * N_DEEP - 1, N_WIDE * N_DEEP)
    after = (after // N_DEEP, lax.rem(after, N_DEEP))
    before = (before // N_DEEP, lax.rem(before, N_DEEP))

    x, y_low, core = wide // 4, lax.rem(wide // 2, 2), lax.rem(wide, 2)

    def place(x_by, y_flip, core_flip):
        return lax.rem(x + x_by, X) * 4 + (1 - y_low if y_flip else y_low) * 2 + (1 - core if core_flip else core)

    other_core = (place(0, False, True), deep)
    other_y = (place(0, True, False), deep)
    x_up = (place(1, False, False), deep)
    x_down = (place(3, False, False), deep)

    barrier = pltpu.get_barrier_semaphore()
    for peer in (after, before, other_core, other_y, x_up, x_down):
        pl.semaphore_signal(barrier, inc=1, device_id=peer, device_id_type=MESH)

    loads = [
        pltpu.make_async_copy(users_in, users, load_sem.at[0]),
        pltpu.make_async_copy(items_in, held.at[0], load_sem.at[1]),
        pltpu.make_async_copy(caps_in, caps_across, load_sem.at[2]),
    ]
    for load in loads:
        load.start()

    def rated_load(stratum):
        columns = pl.ds(pl.multiple_of(stratum * BLOCK, BLOCK), BLOCK)
        return pltpu.make_async_copy(ratings.at[:, columns], rated.at[stratum], rated_sem.at[stratum])

    for stratum in range(STRATA):
        rated_load(stratum).start()

    def item_copy(stratum, chunk):
        rows = pl.ds(chunk * C, C)
        return pltpu.make_async_remote_copy(
            src_ref=leaving.at[stratum, rows],
            dst_ref=held.at[stratum + 1, rows],
            send_sem=item_send.at[stratum, chunk],
            recv_sem=item_recv.at[stratum, chunk],
            device_id=after,
            device_id_type=MESH,
        )

    def prepare(stratum):
        lane = lax.broadcasted_iota(jnp.int32, (USERS, STRATA), 1)
        column = jnp.sum(jnp.where(lane == stratum, caps[...], 0), axis=1, keepdims=True)
        limit[...] = jnp.broadcast_to(column, (USERS, C))

    loads[2].wait()
    caps[...] = caps_across[...].T
    counts = jnp.sum(caps[...], axis=1, keepdims=True).astype(F32)
    confidence[...] = jnp.broadcast_to(lax.rsqrt(counts), (USERS, C))
    loads[0].wait()
    users_high[...], users_low[...] = split(users[...])
    loads[1].wait()

    pl.semaphore_wait(barrier, 6)

    def one_stratum(stratum, carry):
        prepare(stratum)
        rated_load(stratum).wait()
        for chunk in range(CHUNKS):

            @pl.when(stratum > 0)
            def _():
                item_copy(stratum - 1, chunk).wait_recv()

            rows = pl.ds(chunk * C, C)
            items = held[stratum, rows, :]
            items_pair = split(items)
            users_pair = (users_high[...], users_low[...])
            predict = product(users_pair, items_pair, ((1,), (1,)))
            block = rated[stratum, :, rows].astype(F32)
            position = lax.broadcasted_iota(jnp.int32, (USERS, C), 1) + chunk * C
            weighted = jnp.where(position < limit[...], predict - block, 0.0) * confidence[...]
            weighted_pair = split(weighted)
            change = product(weighted_pair, users_pair, ((0,), (0,)))
            leaving[stratum, rows, :] = items - learn_rate * (change + penalty * items)
            item_copy(stratum, chunk).start()
            part = product(weighted_pair, items_pair, ((1,), (0,)))
            gradient[...] = part if chunk == 0 else gradient[...] + part
        old = users[...]
        new = old - learn_rate * (gradient[...] + penalty * old)
        users[...] = new
        users_high[...], users_low[...] = split(new)
        return carry

    lax.fori_loop(0, STRATA, one_stratum, 0)

    stores = []

    def store(source, target):
        copy = pltpu.make_async_copy(source, target, store_sem.at[len(stores)])
        copy.start()
        stores.append(copy)

    new = users[...]
    high, rest = users_high[...], new - users_high[...].astype(F32)
    middle = rest.astype(BF16)
    low = (rest - middle.astype(F32)).astype(BF16)
    chosen = (lax.broadcasted_iota(jnp.int32, (USERS, REFRESH), 0) == ids[...]).astype(F32).astype(BF16)
    pick = functools.partial(
        lax.dot_general, chosen, dimension_numbers=(((0,), (0,)), ((), ())), preferred_element_type=F32
    )
    picked[wide] = pick(high) + (pick(middle) + pick(low))

    sent = []

    def give(slot, kind, peer, half=None):
        rows = pl.ds(0, REFRESH) if half is None else pl.ds(half * (REFRESH // 2), REFRESH // 2)
        copy = pltpu.make_async_remote_copy(
            src_ref=picked.at[slot, rows],
            dst_ref=picked.at[slot, rows],
            send_sem=pick_send.at[len(sent)],
            recv_sem=pick_recv.at[kind],
            device_id=peer,
            device_id_type=MESH,
        )
        copy.start()
        sent.append(copy)

    def take(slot, kind, half=None):
        rows = pl.ds(0, REFRESH) if half is None else pl.ds(half * (REFRESH // 2), REFRESH // 2)
        pltpu.make_async_remote_copy(
            src_ref=picked.at[slot, rows],
            dst_ref=picked.at[slot, rows],
            send_sem=pick_send.at[0],
            recv_sem=pick_recv.at[kind],
            device_id=other_core,
            device_id_type=MESH,
        ).wait_recv()

    def keep(slot):
        store(picked.at[slot], picked_out.at[pl.ds(pl.multiple_of(slot * REFRESH, REFRESH), REFRESH)])

    OTHER_Y, FROM_DOWN, FROM_UP, HALF_DOWN, HALF_UP, CORE = 0, 1, 3, 5, 7, 9
    give(wide, OTHER_Y, other_y)
    give(wide, FROM_DOWN, x_up)
    give(wide, FROM_UP, x_down)
    give(wide, CORE, other_core)
    store(users, users_out)
    keep(wide)

    slot = place(0, True, False)
    take(slot, OTHER_Y)
    give(slot, FROM_DOWN + 1, x_up)
    give(slot, FROM_UP + 1, x_down)
    give(slot, CORE + 1, other_core)
    keep(slot)

    for v in (0, 1):
        down, up = place(3, v == 1, False), place(1, v == 1, False)
        take(down, FROM_DOWN + v)
        give(down, HALF_DOWN + v, x_up, half=0)
        give(down, CORE + 2 + v, other_core)
        keep(down)
        take(up, FROM_UP + v)
        give(up, HALF_UP + v, x_down, half=1)
        give(up, CORE + 4 + v, other_core)
        keep(up)

    for v in (0, 1):
        far = place(2, v == 1, False)
        take(far, HALF_DOWN + v, half=0)
        take(far, HALF_UP + v, half=1)
        give(far, CORE + 6 + v, other_core)
        keep(far)

    for order, slot in enumerate(
        (
            place(0, False, True), place(0, True, True),
            place(3, False, True), place(3, True, True),
            place(1, False, True), place(1, True, True),
            place(2, False, True), place(2, True, True),
        )
    ):
        take(slot, CORE + order)
        keep(slot)

    for chunk in range(CHUNKS):
        rows = pl.ds(chunk * C, C)
        item_copy(STRATA - 1, chunk).wait_recv()
        store(held.at[STRATA, rows], items_out.at[rows])

    def drain(stratum, carry):
        for chunk in range(CHUNKS):
            item_copy(stratum, chunk).wait_send()
        return carry

    lax.fori_loop(0, STRATA, drain, 0)
    for copy in sent:
        copy.wait_send()
    for copy in stores:
        copy.wait()


def run_strata(ratings, caps, users, items, ids):
    sends, kinds, stores = 4 + 3 + 8 + 2, 17, 1 + 16 + CHUNKS
    anywhere = pl.BlockSpec(memory_space=pl.ANY)
    return pl.pallas_call(
        strata_kernel,
        out_shape=(
            jax.ShapeDtypeStruct((USERS, RANK), F32),
            jax.ShapeDtypeStruct((BLOCK, RANK), F32),
            jax.ShapeDtypeStruct((N_WIDE * REFRESH, RANK), F32),
        ),
        in_specs=[anywhere, anywhere, anywhere, anywhere, pl.BlockSpec(memory_space=pltpu.VMEM)],
        out_specs=(anywhere, anywhere, anywhere),
        scratch_shapes=[
            pltpu.VMEM((STRATA, USERS, BLOCK), BF16),
            pltpu.VMEM((STRATA, USERS), jnp.int32),
            pltpu.VMEM((USERS, STRATA), jnp.int32),
            pltpu.VMEM((USERS, RANK), F32),
            pltpu.VMEM((USERS, RANK), BF16),
            pltpu.VMEM((USERS, RANK), BF16),
            pltpu.VMEM((USERS, RANK), F32),
            pltpu.VMEM((STRATA + 1, BLOCK, RANK), F32),
            pltpu.VMEM((STRATA, BLOCK, RANK), F32),
            pltpu.VMEM((N_WIDE, REFRESH, RANK), F32),
            pltpu.VMEM((USERS, C), jnp.int32),
            pltpu.VMEM((USERS, C), F32),
            pltpu.SemaphoreType.DMA((3,)),
            pltpu.SemaphoreType.DMA((STRATA,)),
            pltpu.SemaphoreType.DMA((STRATA, CHUNKS)),
            pltpu.SemaphoreType.DMA((STRATA, CHUNKS)),
            pltpu.SemaphoreType.DMA((sends,)),
            pltpu.SemaphoreType.DMA((kinds,)),
            pltpu.SemaphoreType.DMA((stores,)),
        ],
        compiler_params=pltpu.CompilerParams(
            collective_id=0, has_side_effects=True, vmem_limit_bytes=VMEM_BYTES
        ),
    )(ratings, caps, users, items, ids)


def scores_kernel(picked, items, users_part, items_part, scores, users_out, items_out, items_high, items_low):
    @pl.when(pl.program_id(0) == 0)
    def _():
        items_high[...], items_low[...] = split(items[...])

    scores[...] = product(split(picked[...]), (items_high[...], items_low[...]), ((1,), (1,)))
    users_out[...] = users_part[...]
    items_out[...] = items_part[...]


def run_scores(picked, users, items):
    steps = 8
    rows = N_WIDE * REFRESH // steps
    part = pl.BlockSpec((USERS // steps, RANK), lambda i: (i, 0))
    return pl.pallas_call(
        scores_kernel,
        grid=(steps,),
        out_shape=(
            jax.ShapeDtypeStruct((N_WIDE * REFRESH, BLOCK), F32),
            jax.ShapeDtypeStruct((USERS, RANK), F32),
            jax.ShapeDtypeStruct((BLOCK, RANK), F32),
        ),
        in_specs=[
            pl.BlockSpec((rows, RANK), lambda i: (i, 0)),
            pl.BlockSpec((BLOCK, RANK), lambda i: (0, 0)),
            part,
            part,
        ],
        out_specs=(pl.BlockSpec((rows, BLOCK), lambda i: (i, 0)), part, part),
        scratch_shapes=[pltpu.VMEM((BLOCK, RANK), BF16), pltpu.VMEM((BLOCK, RANK), BF16)],
    )(picked, items, users, items)


def per_device(ratings, recency_caps, user_factors, item_factors, refresh_ids):
    users, items, picked = run_strata(
        ratings, recency_caps.T, user_factors, item_factors, refresh_ids.reshape(1, REFRESH)
    )
    scores, users, items = run_scores(picked, users, items)
    return (users, items, scores[None])


def solution(mesh):
    placed = (
        P(("wide", "deep"), None),
        P(("wide", "deep"), None),
        P(("wide", "deep"), None),
        P(("wide", "deep"), None),
        P(("wide", "deep")),
    )
    return jax.shard_map(
        per_device,
        mesh=mesh,
        in_specs=placed,
        out_specs=(P(("wide", "deep"), None), P(("wide", "deep"), None), P("deep", None, "wide")),
        check_vma=False,
    )
```

profile of v0, /device:TPU:1, one launch (start us, length us, event | category | flops | bytes accessed | tf_op | source)
XLA Modules:
  0.0 126.5 jit_solution(11101219752612093096)
XLA Ops:
  0.6 117.9 %shard_map.76 = (f32[512,256]{1,0:T(8,128)}, f32[512,256]{1,0:T(8,128)}, f32[2048,256]{1,0:T(8,128)}) custom-call(bf16[512,4096]{1,0:T(8,128)(2,1)} %ratings.1, s32[8,512]{1,0:T(8,128)} %bitcast.3, f32[512,256]{1,0:T(8,128)} %users_in.1, f32[512,256]{1,0:T(8,128)} %items_in.1, s32[1,128]{1,0:T(1,128)} %bitcast.4), custom_call_target="tpu_custom_call" | custom-call | tf_op jit(solution)/shard_map/pallas_call | solution.py:251
  118.5 8.0 %shard_map.77 = (f32[2048,512]{1,0:T(8,128)}, f32[512,256]{1,0:T(8,128)}, f32[512,256]{1,0:T(8,128)}) custom-call(f32[2048,256]{1,0:T(8,128)} %get-tuple-element.9.picked, f32[512,256]{1,0:T(8,128)} %get-tuple-element.10.items.items_part, f32[512,256]{1,0:T(8,128)} %get-tuple-element.11.users_part, f32[512,256]{1,0:T(8,128)} %get-tuple-element.10.items.items_part), custom_call_target="tpu_custom_call" | custom-call | tf_op jit(solution)/shard_map/pallas_call | solution.py:301
where the time goes:
time: 127 us
  Pallas kernels  126 us (99%)
    pallas_call x1, Pallas kernels, run_strata(): pl.pallas_call(strata_kernel, out_shape=(jax.ShapeDtypeStruct((USERS, RAN...  118 us
    pallas_call x1, Pallas kernels, run_scores(): pl.pallas_call(scores_kernel, grid=(steps,), out_shape=(jax.ShapeDtypeStr...  8 us

commit v1 on v0

v1 whole, which is shorter than its diff:
```python
import functools

import jax
import jax.numpy as jnp
from jax import lax
from jax.experimental import pallas as pl
from jax.experimental.pallas import tpu as pltpu
from jax.sharding import PartitionSpec as P

STRATA = 8
USERS = 512
BLOCK = 512
RANK = 256
REFRESH = 128
N_WIDE = 16
N_DEEP = 16
X = 4
CHUNKS = 4
C = BLOCK // CHUNKS

VMEM_BYTES = 44 * 2**20
PARTS = 4
HOLD = 2
HALF = REFRESH // 2
PART_ROWS = N_WIDE * REFRESH // PARTS

learn_rate = 0.1
penalty = 0.05

MESH = pl.DeviceIdType.MESH
F32 = jnp.float32
BF16 = jnp.bfloat16


def split(value):
    high = value.astype(BF16)
    return high, (value - high.astype(F32)).astype(BF16)


def product(left, right, dims):
    numbers = ((dims[0], dims[1]), ((), ()))
    dot = functools.partial(lax.dot_general, dimension_numbers=numbers, preferred_element_type=F32)
    return dot(left[0], right[0]) + (dot(left[0], right[1]) + dot(left[1], right[0]))


def strata_kernel(
    ratings, caps_in, users_in, items_in, ids,
    users_out, items_out, picked,
    rated, caps_across, caps, users, users_high, users_low, gradient, held, leaving, chosen, limit, confidence,
    load_sem, rated_sem, item_send, item_recv, last_recv, pick_send, pick_recv,
):
    wide, deep = lax.axis_index("wide"), lax.axis_index("deep")
    joined = wide * N_DEEP + deep
    after = lax.rem(joined + 1, N_WIDE * N_DEEP)
    before = lax.rem(joined + N_WIDE * N_DEEP - 1, N_WIDE * N_DEEP)
    after = (after // N_DEEP, lax.rem(after, N_DEEP))
    before = (before // N_DEEP, lax.rem(before, N_DEEP))

    x, y_low, core = wide // 4, lax.rem(wide // 2, 2), lax.rem(wide, 2)

    def place(x_by, y_flip, core_flip):
        return lax.rem(x + x_by, X) * 4 + (1 - y_low if y_flip else y_low) * 2 + (1 - core if core_flip else core)

    other_core = (place(0, False, True), deep)
    other_y = (place(0, True, False), deep)
    x_up = (place(1, False, False), deep)
    x_down = (place(3, False, False), deep)

    barrier = pltpu.get_barrier_semaphore()
    for peer in (after, before, other_core, other_y, x_up, x_down):
        pl.semaphore_signal(barrier, inc=1, device_id=peer, device_id_type=MESH)

    loads = [
        pltpu.make_async_copy(users_in, users, load_sem.at[0]),
        pltpu.make_async_copy(items_in, held.at[0], load_sem.at[1]),
        pltpu.make_async_copy(caps_in, caps_across, load_sem.at[2]),
    ]
    for load in loads:
        load.start()

    def rated_load(stratum):
        columns = pl.ds(pl.multiple_of(stratum * BLOCK, BLOCK), BLOCK)
        return pltpu.make_async_copy(ratings.at[:, columns], rated.at[stratum], rated_sem.at[stratum])

    for stratum in range(STRATA):
        rated_load(stratum).start()

    def item_copy(stratum, chunk):
        rows = pl.ds(chunk * C, C)
        return pltpu.make_async_remote_copy(
            src_ref=leaving.at[stratum, rows],
            dst_ref=held.at[stratum + 1, rows],
            send_sem=item_send.at[stratum, chunk],
            recv_sem=item_recv.at[stratum, chunk],
            device_id=after,
            device_id_type=MESH,
        )

    def last_item_copy(chunk):
        rows = pl.ds(chunk * C, C)
        return pltpu.make_async_remote_copy(
            src_ref=leaving.at[STRATA - 1, rows],
            dst_ref=items_out.at[rows],
            send_sem=item_send.at[STRATA - 1, chunk],
            recv_sem=last_recv.at[chunk],
            device_id=after,
            device_id_type=MESH,
        )

    def prepare(stratum):
        lane = lax.broadcasted_iota(jnp.int32, (USERS, STRATA), 1)
        column = jnp.sum(jnp.where(lane == stratum, caps[...], 0), axis=1, keepdims=True)
        limit[...] = jnp.broadcast_to(column, (USERS, C))

    loads[2].wait()
    caps[...] = caps_across[...].T
    counts = jnp.sum(caps[...], axis=1, keepdims=True).astype(F32)
    confidence[...] = jnp.broadcast_to(lax.rsqrt(counts), (USERS, C))
    loads[0].wait()
    users_high[...], users_low[...] = split(users[...])
    loads[1].wait()

    row = lax.broadcasted_iota(jnp.int32, (USERS, REFRESH), 0)
    chosen[...] = (row == ids[...]).astype(F32).T.astype(BF16)
    prepare(0)
    pl.semaphore_wait(barrier, 6)

    def weigh(stratum, chunk):
        rows = pl.ds(chunk * C, C)
        items_pair = split(held[stratum, rows, :])
        predict = product((users_high[...], users_low[...]), items_pair, ((1,), (1,)))
        block = rated[stratum, :, rows].astype(F32)
        position = lax.broadcasted_iota(jnp.int32, (USERS, C), 1) + chunk * C
        weighted = jnp.where(position < limit[...], predict - block, 0.0) * confidence[...]
        return split(weighted), items_pair

    def update_items(stratum, chunk, weighted_pair, users_pair):
        rows = pl.ds(chunk * C, C)
        items = held[stratum, rows, :]
        change = product(weighted_pair, users_pair, ((0,), (0,)))
        leaving[stratum, rows, :] = items - learn_rate * (change + penalty * items)

    def add_gradient(chunk, weighted_pair, items_pair):
        part = product(weighted_pair, items_pair, ((1,), (0,)))
        gradient[...] = part if chunk == 0 else gradient[...] + part

    def next_users():
        old = users[...]
        return old - learn_rate * (gradient[...] + penalty * old)

    def one_stratum(stratum, carry):
        rated_load(stratum).wait()
        for chunk in range(CHUNKS):

            @pl.when(stratum > 0)
            def _():
                item_copy(stratum - 1, chunk).wait_recv()

            weighted_pair, items_pair = weigh(stratum, chunk)
            update_items(stratum, chunk, weighted_pair, (users_high[...], users_low[...]))
            item_copy(stratum, chunk).start()
            add_gradient(chunk, weighted_pair, items_pair)
        new = next_users()
        users[...] = new
        users_high[...], users_low[...] = split(new)
        prepare(stratum + 1)
        return carry

    lax.fori_loop(0, STRATA - 1, one_stratum, 0)

    final = STRATA - 1
    rated_load(final).wait()
    waiting = []
    for chunk in range(CHUNKS):
        item_copy(final - 1, chunk).wait_recv()
        weighted_pair, items_pair = weigh(final, chunk)
        if chunk < CHUNKS - HOLD:
            update_items(final, chunk, weighted_pair, (users_high[...], users_low[...]))
            last_item_copy(chunk).start()
        else:
            waiting.append((chunk, weighted_pair))
        add_gradient(chunk, weighted_pair, items_pair)
    new = next_users()
    high, low = split(new)
    lowest = (new - high.astype(F32) - low.astype(F32)).astype(BF16)
    pick = functools.partial(lax.dot_general, dimension_numbers=(((1,), (0,)), ((), ())), preferred_element_type=F32)
    picked[wide] = pick(chosen[...], high) + (pick(chosen[...], low) + pick(chosen[...], lowest))

    sent = []

    def piece(slot, half):
        return picked.at[slot] if half is None else picked.at[slot, pl.ds(half * HALF, HALF)]

    def move(slot, half, kind, peer, number):
        return pltpu.make_async_remote_copy(
            src_ref=piece(slot, half),
            dst_ref=piece(slot, half),
            send_sem=pick_send.at[number],
            recv_sem=pick_recv.at[kind],
            device_id=peer,
            device_id_type=MESH,
        )

    def give(slot, half, kind, peer):
        copy = move(slot, half, kind, peer, len(sent))
        copy.start()
        sent.append(copy)

    def take(slot, half, kind):
        move(slot, half, kind, other_core, 0).wait_recv()

    def other_y_kind(half):
        return half

    def near_kind(v, from_up, half):
        return 2 + (v * 2 + from_up) * 2 + half

    def far_kind(v, half):
        return 10 + v * 2 + half

    def core_kind(order):
        return 14 + order

    for half in (0, 1):
        give(wide, half, other_y_kind(half), other_y)
        give(wide, half, near_kind(0, 0, half), x_up)
        give(wide, half, near_kind(0, 1, half), x_down)
    give(wide, None, core_kind(0), other_core)

    for chunk, weighted_pair in waiting:
        update_items(final, chunk, weighted_pair, (users_high[...], users_low[...]))
        last_item_copy(chunk).start()
    users_out[...] = new

    beside = place(0, True, False)
    down, up = place(3, False, False), place(1, False, False)
    beside_down, beside_up = place(3, True, False), place(1, True, False)
    for half in (0, 1):
        take(beside, half, other_y_kind(half))
        give(beside, half, near_kind(1, 0, half), x_up)
        give(beside, half, near_kind(1, 1, half), x_down)
        take(down, half, near_kind(0, 0, half))
        if half == 0:
            give(down, 0, far_kind(0, 0), x_up)
        take(up, half, near_kind(0, 1, half))
        if half == 1:
            give(up, 1, far_kind(0, 1), x_down)
    give(beside, None, core_kind(1), other_core)
    give(down, None, core_kind(2), other_core)
    give(up, None, core_kind(3), other_core)
    for half in (0, 1):
        take(beside_down, half, near_kind(1, 0, half))
        if half == 0:
            give(beside_down, 0, far_kind(1, 0), x_up)
        take(beside_up, half, near_kind(1, 1, half))
        if half == 1:
            give(beside_up, 1, far_kind(1, 1), x_down)
    give(beside_down, None, core_kind(4), other_core)
    give(beside_up, None, core_kind(5), other_core)
    for v in (0, 1):
        opposite = place(2, v == 1, False)
        for half in (0, 1):
            take(opposite, half, far_kind(v, half))
            give(opposite, half, core_kind(6 + 2 * v + half), other_core)

    for chunk in range(CHUNKS):
        last_item_copy(chunk).wait_recv()

    for order, slot in enumerate(
        (
            place(0, False, True), place(0, True, True),
            place(3, False, True), place(1, False, True),
            place(3, True, True), place(1, True, True),
        )
    ):
        take(slot, None, core_kind(order))
    for v in (0, 1):
        for half in (0, 1):
            take(place(2, v == 1, True), half, core_kind(6 + 2 * v + half))

    def drain(stratum, carry):
        for chunk in range(CHUNKS):
            item_copy(stratum, chunk).wait_send()
        return carry

    lax.fori_loop(0, STRATA - 1, drain, 0)
    for chunk in range(CHUNKS):
        last_item_copy(chunk).wait_send()
    for copy in sent:
        copy.wait_send()


def run_strata(ratings, caps, users, items, ids):
    sends, kinds = 27, 24
    far, here = pl.BlockSpec(memory_space=pltpu.HBM), pl.BlockSpec(memory_space=pltpu.VMEM)
    return pl.pallas_call(
        strata_kernel,
        out_shape=(
            jax.ShapeDtypeStruct((USERS, RANK), F32),
            jax.ShapeDtypeStruct((BLOCK, RANK), F32),
            jax.ShapeDtypeStruct((N_WIDE, REFRESH, RANK), F32),
        ),
        in_specs=[far, far, far, far, here],
        out_specs=(here, here, here),
        scratch_shapes=[
            pltpu.VMEM((STRATA, USERS, BLOCK), BF16),
            pltpu.VMEM((STRATA, USERS), jnp.int32),
            pltpu.VMEM((USERS, STRATA), jnp.int32),
            pltpu.VMEM((USERS, RANK), F32),
            pltpu.VMEM((USERS, RANK), BF16),
            pltpu.VMEM((USERS, RANK), BF16),
            pltpu.VMEM((USERS, RANK), F32),
            pltpu.VMEM((STRATA, BLOCK, RANK), F32),
            pltpu.VMEM((STRATA, BLOCK, RANK), F32),
            pltpu.VMEM((REFRESH, USERS), BF16),
            pltpu.VMEM((USERS, C), jnp.int32),
            pltpu.VMEM((USERS, C), F32),
            pltpu.SemaphoreType.DMA((3,)),
            pltpu.SemaphoreType.DMA((STRATA,)),
            pltpu.SemaphoreType.DMA((STRATA, CHUNKS)),
            pltpu.SemaphoreType.DMA((STRATA - 1, CHUNKS)),
            pltpu.SemaphoreType.DMA((CHUNKS,)),
            pltpu.SemaphoreType.DMA((sends,)),
            pltpu.SemaphoreType.DMA((kinds,)),
        ],
        compiler_params=pltpu.CompilerParams(
            collective_id=0, has_side_effects=True, vmem_limit_bytes=VMEM_BYTES
        ),
    )(ratings, caps, users, items, ids)


def scores_kernel(picked, items, users, scores, users_out, items_out, right, staged, store_sem):
    passed = [
        pltpu.make_async_copy(users, users_out, store_sem.at[0]),
        pltpu.make_async_copy(items, items_out, store_sem.at[1]),
    ]
    for copy in passed:
        copy.start()
    high, low = split(items[...].T)
    right[0:RANK, :], right[RANK : 2 * RANK, :], right[2 * RANK :, :] = high, low, high
    stores = []
    for part in range(PARTS):
        rows = pl.ds(part * PART_ROWS, PART_ROWS)
        high, low = split(picked[rows, :])
        left = jnp.concatenate([high, high, low], axis=1)
        staged[rows, :] = jnp.dot(left, right[...], preferred_element_type=F32)
        copy = pltpu.make_async_copy(staged.at[rows], scores.at[rows], store_sem.at[2 + part])
        copy.start()
        stores.append(copy)
    for copy in passed + stores:
        copy.wait()


def run_scores(picked, users, items):
    here = pl.BlockSpec(memory_space=pltpu.VMEM)
    anywhere = pl.BlockSpec(memory_space=pl.ANY)
    return pl.pallas_call(
        scores_kernel,
        out_shape=(
            jax.ShapeDtypeStruct((N_WIDE * REFRESH, BLOCK), F32),
            jax.ShapeDtypeStruct((USERS, RANK), F32),
            jax.ShapeDtypeStruct((BLOCK, RANK), F32),
        ),
        in_specs=[here, here, here],
        out_specs=(anywhere, anywhere, anywhere),
        scratch_shapes=[
            pltpu.VMEM((3 * RANK, BLOCK), BF16),
            pltpu.VMEM((N_WIDE * REFRESH, BLOCK), F32),
            pltpu.SemaphoreType.DMA((2 + PARTS,)),
        ],
        compiler_params=pltpu.CompilerParams(vmem_limit_bytes=32 * 2**20),
    )(picked, items, users)


def per_device(ratings, recency_caps, user_factors, item_factors, refresh_ids):
    inputs = (ratings, recency_caps.T, user_factors, item_factors, refresh_ids.reshape(1, REFRESH))
    inputs = [pltpu.with_memory_space_constraint(value, pltpu.HBM) for value in inputs]
    users, items, picked = run_strata(*inputs)
    scores, users, items = run_scores(picked.reshape(N_WIDE * REFRESH, RANK), users, items)
    return (users, items, scores[None])


def solution(mesh):
    placed = (
        P(("wide", "deep"), None),
        P(("wide", "deep"), None),
        P(("wide", "deep"), None),
        P(("wide", "deep"), None),
        P(("wide", "deep")),
    )
    return jax.shard_map(
        per_device,
        mesh=mesh,
        in_specs=placed,
        out_specs=(P(("wide", "deep"), None), P(("wide", "deep"), None), P("deep", None, "wide")),
        check_vma=False,
    )
```

time: 127 us -> 116 us (0.913); the launches traced: 127 us -> 114 us
  Pallas kernels: 126 us -> 113 us
    pallas_call x1, Pallas kernels: 118 us -> 110 us  [run_strata(): pl.pallas_call(strata_kernel, out_shape=(jax.ShapeDtypeStruct((USERS, RAN...]
    pallas_call x1, Pallas kernels: 8 us -> 2.99 us  [run_scores(): pl.pallas_call(scores_kernel, out_shape=(jax.ShapeDtypeStruct((N_WIDE * R...]
where the time goes in v1:
time: 116 us; the launch traced here: 114 us
  Pallas kernels  113 us (97%)
    pallas_call x1, Pallas kernels, run_strata(): pl.pallas_call(strata_kernel, out_shape=(jax.ShapeDtypeStruct((USERS, RAN...  110 us
    pallas_call x1, Pallas kernels, run_scores(): pl.pallas_call(scores_kernel, out_shape=(jax.ShapeDtypeStruct((N_WIDE * R...  2.99 us

profile of v1, /device:TPU:1, one launch (start us, length us, event | category | flops | bytes accessed | tf_op | source)
XLA Modules:
  0.0 113.7 jit_solution(10359299880708810910)
XLA Ops:
  0.6 110.1 %shard_map.76 = (f32[512,256]{1,0:T(8,128)S(1)}, f32[512,256]{1,0:T(8,128)S(1)}, f32[16,128,256]{2,1,0:T(8,128)S(1)}) custom-call(bf16[512,4096]{1,0:T(8,128)(2,1)} %ratings.1, s32[8,512]{1,0:T(8,128)} %bitcast.5, f32[512,256]{1,0:T(8,128)} %users_in.1, f32[512,256]{1,0:T(8,128)} %items_in.1, s32[1,128]{1,0:T(1,128)} %bitcast.6), custom_call_target="tpu_custom_call" | custom-call | tf_op jit(solution)/shard_map/pallas_call | solution.py:296
  110.7 3.0 %shard_map.77 = (f32[2048,512]{1,0:T(8,128)}, f32[512,256]{1,0:T(8,128)}, f32[512,256]{1,0:T(8,128)}) custom-call(f32[2048,256]{1,0:T(8,128)S(1)} %bitcast.4, f32[512,256]{1,0:T(8,128)S(1)} %get-tuple-element.10.items, f32[512,256]{1,0:T(8,128)S(1)} %get-tuple-element.11.users), custom_call_target="tpu_custom_call" | custom-call | tf_op jit(solution)/shard_map/pallas_call | solution.py:357

commit v2 on v1

--- a/solution.py
+++ b/solution.py
@@ -82,8 +82,7 @@
         columns = pl.ds(pl.multiple_of(stratum * BLOCK, BLOCK), BLOCK)
         return pltpu.make_async_copy(ratings.at[:, columns], rated.at[stratum], rated_sem.at[stratum])
 
-    for stratum in range(STRATA):
-        rated_load(stratum).start()
+    rated_load(0).start()
 
     def item_copy(stratum, chunk):
         rows = pl.ds(chunk * C, C)
@@ -120,8 +119,6 @@
     users_high[...], users_low[...] = split(users[...])
     loads[1].wait()
 
-    row = lax.broadcasted_iota(jnp.int32, (USERS, REFRESH), 0)
-    chosen[...] = (row == ids[...]).astype(F32).T.astype(BF16)
     prepare(0)
     pl.semaphore_wait(barrier, 6)
 
@@ -160,10 +157,18 @@
             update_items(stratum, chunk, weighted_pair, (users_high[...], users_low[...]))
             item_copy(stratum, chunk).start()
             add_gradient(chunk, weighted_pair, items_pair)
+            if chunk == 0:
+                rated_load(stratum + 1).start()
         new = next_users()
         users[...] = new
         users_high[...], users_low[...] = split(new)
         prepare(stratum + 1)
+
+        @pl.when(stratum == 0)
+        def _():
+            row = lax.broadcasted_iota(jnp.int32, (USERS, REFRESH), 0)
+            chosen[...] = (row == ids[...]).astype(F32).T.astype(BF16)
+
         return carry
 
     lax.fori_loop(0, STRATA - 1, one_stratum, 0)

time: 116 us -> 116 us (level)
  no operation moved by 1% of the time
where the time goes in v2:
time: 116 us; the launch traced here: 114 us
  Pallas kernels  113 us (97%)
    pallas_call x1, Pallas kernels, run_strata(): pl.pallas_call(strata_kernel, out_shape=(jax.ShapeDtypeStruct((USERS, RAN...  110 us
    pallas_call x1, Pallas kernels, run_scores(): pl.pallas_call(scores_kernel, out_shape=(jax.ShapeDtypeStruct((N_WIDE * R...  2.99 us

profile of v2, /device:TPU:1, one launch (start us, length us, event | category | flops | bytes accessed | tf_op | source)
XLA Modules:
  0.0 113.8 jit_solution(8883778850556667835)
XLA Ops:
  0.6 110.2 %shard_map.76 = (f32[512,256]{1,0:T(8,128)S(1)}, f32[512,256]{1,0:T(8,128)S(1)}, f32[16,128,256]{2,1,0:T(8,128)S(1)}) custom-call(bf16[512,4096]{1,0:T(8,128)(2,1)} %ratings.1, s32[8,512]{1,0:T(8,128)} %bitcast.5, f32[512,256]{1,0:T(8,128)} %users_in.1, f32[512,256]{1,0:T(8,128)} %items_in.1, s32[1,128]{1,0:T(1,128)} %bitcast.6), custom_call_target="tpu_custom_call" | custom-call | tf_op jit(solution)/shard_map/pallas_call | solution.py:301
  110.8 3.0 %shard_map.77 = (f32[2048,512]{1,0:T(8,128)}, f32[512,256]{1,0:T(8,128)}, f32[512,256]{1,0:T(8,128)}) custom-call(f32[2048,256]{1,0:T(8,128)S(1)} %bitcast.4, f32[512,256]{1,0:T(8,128)S(1)} %get-tuple-element.10.items, f32[512,256]{1,0:T(8,128)S(1)} %get-tuple-element.11.users), custom_call_target="tpu_custom_call" | custom-call | tf_op jit(solution)/shard_map/pallas_call | solution.py:362

commit v3 on v2

--- a/solution.py
+++ b/solution.py
@@ -19,7 +19,7 @@
 C = BLOCK // CHUNKS
 
 VMEM_BYTES = 44 * 2**20
-PARTS = 4
+PARTS = 8
 HOLD = 2
 HALF = REFRESH // 2
 PART_ROWS = N_WIDE * REFRESH // PARTS
@@ -45,8 +45,8 @@
 
 def strata_kernel(
     ratings, caps_in, users_in, items_in, ids,
-    users_out, items_out, picked,
-    rated, caps_across, caps, users, users_high, users_low, gradient, held, leaving, chosen, limit, confidence,
+    users_out, items_out, picked_high, picked_low, right,
+    rated, caps_across, caps, users, users_high, users_low, gradient, held, leaving, chosen, picked, limit, confidence,
     load_sem, rated_sem, item_send, item_recv, last_recv, pick_send, pick_recv,
 ):
     wide, deep = lax.axis_index("wide"), lax.axis_index("deep")
@@ -211,6 +211,11 @@
         copy.start()
         sent.append(copy)
 
+    def ready(slot, half=None):
+        start, length = (0, REFRESH) if half is None else (half * HALF, HALF)
+        rows = pl.ds(pl.multiple_of(slot * REFRESH + start, HALF), length)
+        picked_high[rows, :], picked_low[rows, :] = split(piece(slot, half)[...])
+
     def take(slot, half, kind):
         move(slot, half, kind, other_core, 0).wait_recv()
 
@@ -236,6 +241,7 @@
         update_items(final, chunk, weighted_pair, (users_high[...], users_low[...]))
         last_item_copy(chunk).start()
     users_out[...] = new
+    ready(wide)
 
     beside = place(0, True, False)
     down, up = place(3, False, False), place(1, False, False)
@@ -253,6 +259,9 @@
     give(beside, None, core_kind(1), other_core)
     give(down, None, core_kind(2), other_core)
     give(up, None, core_kind(3), other_core)
+    ready(beside)
+    ready(down)
+    ready(up)
     for half in (0, 1):
         take(beside_down, half, near_kind(1, 0, half))
         if half == 0:
@@ -262,14 +271,20 @@
             give(beside_up, 1, far_kind(1, 1), x_down)
     give(beside_down, None, core_kind(4), other_core)
     give(beside_up, None, core_kind(5), other_core)
+    ready(beside_down)
+    ready(beside_up)
     for v in (0, 1):
         opposite = place(2, v == 1, False)
         for half in (0, 1):
             take(opposite, half, far_kind(v, half))
             give(opposite, half, core_kind(6 + 2 * v + half), other_core)
+            ready(opposite, half)
 
     for chunk in range(CHUNKS):
         last_item_copy(chunk).wait_recv()
+        columns = pl.ds(chunk * C, C)
+        high, low = split(items_out[columns, :].T)
+        right[0:RANK, columns], right[RANK : 2 * RANK, columns], right[2 * RANK :, columns] = high, low, high
 
     for order, slot in enumerate(
         (
@@ -279,9 +294,11 @@
         )
     ):
         take(slot, None, core_kind(order))
+        ready(slot)
     for v in (0, 1):
         for half in (0, 1):
             take(place(2, v == 1, True), half, core_kind(6 + 2 * v + half))
+            ready(place(2, v == 1, True), half)
 
     def drain(stratum, carry):
         for chunk in range(CHUNKS):
@@ -303,10 +320,12 @@
         out_shape=(
             jax.ShapeDtypeStruct((USERS, RANK), F32),
             jax.ShapeDtypeStruct((BLOCK, RANK), F32),
-            jax.ShapeDtypeStruct((N_WIDE, REFRESH, RANK), F32),
+            jax.ShapeDtypeStruct((N_WIDE * REFRESH, RANK), BF16),
+            jax.ShapeDtypeStruct((N_WIDE * REFRESH, RANK), BF16),
+            jax.ShapeDtypeStruct((3 * RANK, BLOCK), BF16),
         ),
         in_specs=[far, far, far, far, here],
-        out_specs=(here, here, here),
+        out_specs=(here,) * 5,
         scratch_shapes=[
             pltpu.VMEM((STRATA, USERS, BLOCK), BF16),
             pltpu.VMEM((STRATA, USERS), jnp.int32),
@@ -318,6 +337,7 @@
             pltpu.VMEM((STRATA, BLOCK, RANK), F32),
             pltpu.VMEM((STRATA, BLOCK, RANK), F32),
             pltpu.VMEM((REFRESH, USERS), BF16),
+            pltpu.VMEM((N_WIDE, REFRESH, RANK), F32),
             pltpu.VMEM((USERS, C), jnp.int32),
             pltpu.VMEM((USERS, C), F32),
             pltpu.SemaphoreType.DMA((3,)),
@@ -334,19 +354,17 @@
     )(ratings, caps, users, items, ids)
 
 
-def scores_kernel(picked, items, users, scores, users_out, items_out, right, staged, store_sem):
+def scores_kernel(picked_high, picked_low, right, items, users, scores, users_out, items_out, staged, store_sem):
     passed = [
         pltpu.make_async_copy(users, users_out, store_sem.at[0]),
         pltpu.make_async_copy(items, items_out, store_sem.at[1]),
     ]
     for copy in passed:
         copy.start()
-    high, low = split(items[...].T)
-    right[0:RANK, :], right[RANK : 2 * RANK, :], right[2 * RANK :, :] = high, low, high
     stores = []
     for part in range(PARTS):
         rows = pl.ds(part * PART_ROWS, PART_ROWS)
-        high, low = split(picked[rows, :])
+        high, low = picked_high[rows, :], picked_low[rows, :]
         left = jnp.concatenate([high, high, low], axis=1)
         staged[rows, :] = jnp.dot(left, right[...], preferred_element_type=F32)
         copy = pltpu.make_async_copy(staged.at[rows], scores.at[rows], store_sem.at[2 + part])
@@ -356,7 +374,7 @@
         copy.wait()
 
 
-def run_scores(picked, users, items):
+def run_scores(picked_high, picked_low, right, users, items):
     here = pl.BlockSpec(memory_space=pltpu.VMEM)
     anywhere = pl.BlockSpec(memory_space=pl.ANY)
     return pl.pallas_call(
@@ -366,22 +384,21 @@
             jax.ShapeDtypeStruct((USERS, RANK), F32),
             jax.ShapeDtypeStruct((BLOCK, RANK), F32),
         ),
-        in_specs=[here, here, here],
+        in_specs=[here] * 5,
         out_specs=(anywhere, anywhere, anywhere),
         scratch_shapes=[
-            pltpu.VMEM((3 * RANK, BLOCK), BF16),
             pltpu.VMEM((N_WIDE * REFRESH, BLOCK), F32),
             pltpu.SemaphoreType.DMA((2 + PARTS,)),
         ],
         compiler_params=pltpu.CompilerParams(vmem_limit_bytes=32 * 2**20),
-    )(picked, items, users)
+    )(picked_high, picked_low, right, items, users)
 
 
 def per_device(ratings, recency_caps, user_factors, item_factors, refresh_ids):
     inputs = (ratings, recency_caps.T, user_factors, item_factors, refresh_ids.reshape(1, REFRESH))
     inputs = [pltpu.with_memory_space_constraint(value, pltpu.HBM) for value in inputs]
-    users, items, picked = run_strata(*inputs)
-    scores, users, items = run_scores(picked.reshape(N_WIDE * REFRESH, RANK), users, items)
+    users, items, picked_high, picked_low, right = run_strata(*inputs)
+    scores, users, items = run_scores(picked_high, picked_low, right, users, items)
     return (users, items, scores[None])
 
 

time: 116 us -> 115 us (level)
  no operation moved by 1% of the time
where the time goes in v3:
time: 115 us; the launch traced here: 114 us
  Pallas kernels  113 us (98%)
    pallas_call x1, Pallas kernels, run_strata(): pl.pallas_call(strata_kernel, out_shape=(jax.ShapeDtypeStruct((USERS, RAN...  110 us
    pallas_call x1, Pallas kernels, run_scores(): pl.pallas_call(scores_kernel, out_shape=(jax.ShapeDtypeStruct((N_WIDE * R...  2.68 us

profile of v3, /device:TPU:1, one launch (start us, length us, event | category | flops | bytes accessed | tf_op | source)
XLA Modules:
  0.0 113.5 jit_solution(5219107057535363025)
XLA Ops:
  0.6 110.2 %shard_map.76 = (f32[512,256]{1,0:T(8,128)S(1)}, f32[512,256]{1,0:T(8,128)S(1)}, bf16[2048,256]{1,0:T(8,128)(2,1)S(1)}, bf16[2048,256]{1,0:T(8,128)(2,1)S(1)}, bf16[768,512]{1,0:T(8,128)(2,1)S(1)}) custom-call(bf16[512,4096]{1,0:T(8,128)(2,1)} %ratings.1, s32[8,512]{1,0:T(8,128)} %bitcast.3, f32[512,256]{1,0:T(8,128)} %users_in.1, f32[512,256]{1,0:T(8,128)} %items_in.1, ...), custom_call_target="tpu_custom_call" | custom-call | tf_op jit(solution)/shard_map/pallas_call | solution.py:318
  110.9 2.7 %shard_map.77 = (f32[2048,512]{1,0:T(8,128)}, f32[512,256]{1,0:T(8,128)}, f32[512,256]{1,0:T(8,128)}) custom-call(bf16[2048,256]{1,0:T(8,128)(2,1)S(1)} %get-tuple-element.11.picked_high, bf16[2048,256]{1,0:T(8,128)(2,1)S(1)} %get-tuple-element.12.picked_low, bf16[768,512]{1,0:T(8,128)(2,1)S(1)} %get-tuple-element.13.right, ...), custom_call_target="tpu_custom_call" | custom-call | tf_op jit(solution)/shard_map/pallas_call | solution.py:380
